TPU v7x, 512 devices: a whole 4x8x8 slice. The times are simulated.
512 devices in a mesh: table: 64 (over z, y), rep: 8 (over x, core).
Axes of the slice: x: 4, y: 8, z: 8, core: 2. Of those that a mesh axis runs over, the one named last changes fastest.
Arguments:
- bag_rows: int32 [512, 1024, 8], P(('table', 'rep')), may hold values from 0 to 2047
- bag_owner: int32 [512, 1024, 8], P(('table', 'rep')), may hold values from 0 to 63, all different within a row; in each aligned block of 1024 rows (0 to 1023, 1024 to 2047, ..., all dimensions but the last counted through in order) at most 192 rows name the same one
- bag_weight: float32 [512, 1024, 8], P(('table', 'rep')), may hold values from 0.25 to 2
- tables: bfloat16 [4, 131072, 128], P(None, 'table'), may hold values from -3 to 3
- returning: int32 [512], P(('table', 'rep')), may hold values 0 or 1
- home: int32 [512], P(('table', 'rep')), may hold values from 0 to 7
- entry: int32 [512], P(('table', 'rep')), may hold values from 0 to 7
- stores: bfloat16 [4096, 30, 512], P(('table', 'rep')), may hold values from -6 to 6
- conv_weight: bfloat16 [4, 1536, 512], P(None, 'table'), may hold values from -0.15625 to 0.15625
- norm_gain: float32 [4, 512], replicated, may hold values from 0.1 to 1.9
Outputs:
- hidden: bfloat16 [512, 1024, 512], P(('table', 'rep'))
Inputs may be any that keep to these rules, and one draw needn't show every extreme that they name: `bag_owner`: the 8 ids of one slot name different owners. Among the slots of one device no owner is named by more than 192 ids, and in some devices' slots one owner is named by exactly 192.
All inputs are finite; a program needn't handle non-finite values. No bound on the sum of `returning` on one device may be relied on, other than what follows from the above.
Results may differ from a plain program's by a relative error of at most 0.0057.
Values may be sent and summed in bfloat16 or wider, within the bound.
A program may use at most 64 MiB of HBM per device.

v0:
```python
import jax
import jax.numpy as jnp
from jax import lax
from jax.sharding import PartitionSpec as P

table_of_id = (0, 1, 2, 2, 3, 3, 3, 3)
bag_bounds = ((0, 1), (1, 2), (2, 4), (4, 8))
epsilon = 1e-05


def pool_bags(weighted):
    sums = [jnp.sum(weighted[..., lower:upper, :], axis=-2) for lower, upper in bag_bounds]
    return jnp.concatenate(sums, axis=-1)


def norm_relu(values, gain):
    mean = jnp.mean(values, axis=-1, keepdims=True)
    centred = values - mean
    spread = jnp.mean(centred * centred, axis=-1, keepdims=True)
    return jnp.maximum(centred * lax.rsqrt(spread + epsilon) * gain, 0.0)


def stack_taps(inputs, carried, offset, dilation):
    span = 2 * dilation
    extended = jnp.concatenate([carried[..., offset : offset + span, :], inputs], axis=-2)
    length = inputs.shape[-2]
    taps = [
        extended[..., span - tap * dilation : span - tap * dilation + length, :] for tap in range(3)
    ]
    return jnp.concatenate(taps, axis=-1)


def local(
    bag_rows, bag_owner, bag_weight, tables, returning, home, entry, stores, conv_weight, norm_gain
):
    owners = lax.axis_size("table")
    samples_here, slot_count, bag_width = bag_rows.shape
    token_count = samples_here * slot_count
    shard_rows = tables.shape[1]
    row_width = tables.shape[2]
    flat_owner = bag_owner.reshape(token_count * bag_width)
    local_rows = (jnp.array(table_of_id, jnp.int32)[None, None, :] * shard_rows + bag_rows).reshape(
        token_count * bag_width
    )
    capacity = min(token_count, (3 * token_count * bag_width + 2 * owners - 1) // (2 * owners))
    onehot = (flat_owner[:, None] == jnp.arange(owners, dtype=jnp.int32)[None, :]).astype(jnp.int32)
    earlier = jnp.cumsum(onehot, axis=0) - onehot
    ranking = jnp.sum(earlier * onehot, axis=1)
    placed = flat_owner * capacity + ranking
    requests = (
        jnp.zeros((owners * capacity,), jnp.int32)
        .at[placed]
        .set(local_rows)
        .reshape(owners, capacity)
    )
    flat_table = tables.reshape(-1, row_width)
    received = lax.all_to_all(requests, "table", split_axis=0, concat_axis=0, tiled=True)
    returned = lax.all_to_all(
        flat_table[received], "table", split_axis=0, concat_axis=0, tiled=True
    )
    picked = returned.reshape(owners * capacity, row_width)[placed].astype(jnp.float32)
    picked = picked * bag_weight.reshape(-1)[:, None]
    block_in = pool_bags(picked.reshape(samples_here, slot_count, bag_width, row_width)).astype(
        jnp.bfloat16
    )
    collected = lax.all_gather(stores, "rep", axis=0, tiled=True)
    carried = collected[home * stores.shape[0] + entry]
    carried = jnp.where(returning[:, None, None] > 0, carried, jnp.zeros_like(carried))
    channels = conv_weight.shape[-1]
    inputs = block_in
    offset = 0
    for layer in range(conv_weight.shape[0]):
        dilation = 2**layer
        stacked = stack_taps(inputs, carried, offset, dilation).reshape(token_count, 3 * channels)
        output = jnp.dot(
            stacked,
            lax.all_gather(conv_weight[layer], "table", axis=0, tiled=True),
            preferred_element_type=jnp.float32,
        )
        active = norm_relu(output, norm_gain[layer]).reshape(samples_here, slot_count, channels)
        offset = offset + 2 * dilation
        if layer % 2 == 0:
            inputs = active.astype(jnp.bfloat16)
        else:
            block_in = (active + block_in.astype(jnp.float32)).astype(jnp.bfloat16)
            inputs = block_in
    return block_in


def solution(mesh):
    in_specs = (
        P(("table", "rep"), None, None),
        P(("table", "rep"), None, None),
        P(("table", "rep"), None, None),
        P(None, "table", None),
        P(("table", "rep")),
        P(("table", "rep")),
        P(("table", "rep")),
        P(("table", "rep"), None, None),
        P(None, "table", None),
        P(),
    )
    out_specs = P(("table", "rep"), None, None)
    return jax.shard_map(local, mesh=mesh, in_specs=in_specs, out_specs=out_specs, check_vma=False)
```

profile of v0, /device:TPU:6, one launch (start us, length us, event | category | flops | bytes accessed | tf_op | source)
XLA Modules:
  0.0 452.4 jit_solution(3087462413247076154)
XLA Ops:
  7.3 1.4 fusion.52
  11.0 1.6 fusion.29
  12.6 36.3 %reduce-window.6 = s32[64,64,128]{2,1,0:T(8,128)} reduce-window(s32[64,64,128]{2,1,0:T(8,128)} %fusion.29, s32[]{:T(128)} %constant.13.clone.1), window={size=1x1x128 pad=0_0x0_0x127_0}, to_apply=%region_0.0 | reduce-window | flops 66584576 | bytes 4194308 | tf_op jit(solution)/shard_map/reduce-window
  48.9 3.3 slice_reduce_fusion.1
  52.5 2.9 broadcast_add_fusion
  55.9 3.5 fusion.28
  60.0 30.5 %scatter_custom_fusion = s32[12288]{0:T(1024)S(1)} fusion(s32[8192]{0:T(1024)S(1)} %bitcast.105, s32[8192]{0:T(1024)S(1)} %reshape.328, s32[]{:T(128)} %constant.13.clone.1), kind=kCustom, calls=%fused_computation.80 | custom fusion | bytes 49156 | tf_op jit(solution)/shard_map/scatter | solution.py:53
  90.6 29.1 %all_to_all.17 = s32[64,1,192]{2,1,0:T(1,128)S(1)} all-to-all(s32[64,1,192]{2,1,0:T(1,128)S(1)} %all_to_all.11), channel_id=1, replica_groups=mesh['table'=64,'rep'=8] {'table'}, dimensions={0} | all-to-all | bytes 98304 | tf_op jit(solution)/shard_map/all_to_all | solution.py:57
  120.0 43.3 %gather_fusion = bf16[12288,128]{1,0:T(8,128)(2,1)} fusion(bf16[8192,128]{1,0:T(8,128)(2,1)S(1)} %bitcast.96, s32[12288]{0:T(1024)S(1)} %broadcast_clamp_fusion), kind=kCustom, calls=%fused_computation | custom fusion | bytes 6340608 | tf_op jit(solution)/shard_map/gather | solution.py:59
  163.3 5.7 %all-to-all-start.1 = ((bf16[64,192,128]{2,1,0:T(8,128)(2,1)}), bf16[64,192,128]{2,1,0:T(8,128)(2,1)}, u32[]{:S(2)}, u32[]{:S(2)}) async-start(bf16[64,192,128]{2,1,0:T(8,128)(2,1)} %bitcast.97), calls=%async_computation.1 | async-start | bytes 6291456 | tf_op jit(solution)/shard_map/all_to_all | solution.py:58
  173.3 71.7 %all-to-all-done.1 = bf16[64,192,128]{2,1,0:T(8,128)(2,1)} async-done(((bf16[64,192,128]{2,1,0:T(8,128)(2,1)}), bf16[64,192,128]{2,1,0:T(8,128)(2,1)}, u32[]{:S(2)}, u32[]{:S(2)}) %all-to-all-start.1) | async-done | bytes 3145760 | tf_op jit(solution)/shard_map/all_to_all | solution.py:58
  245.0 30.5 %gather_fusion.1 = bf16[8192,128]{1,0:T(8,128)(2,1)} fusion(bf16[12288,128]{1,0:T(8,128)(2,1)} %bitcast.6, s32[8192]{0:T(1024)S(1)} %broadcast_clamp_fusion.1), kind=kCustom, calls=%fused_computation.1 | custom fusion | bytes 4227072 | tf_op jit(solution)/shard_map/gather | solution.py:61
  275.5 1.9 bitcast_convert_fusion
  283.4 1.3 slice_dynamic-update-slice_fusion.1
  285.8 4.2 fusion.54
  292.1 3.7 fusion.55
  296.3 1.3 fusion.40
  299.6 51.4 %all-gather.16.cloned.1.call-done = bf16[1,1536,512]{2,1,0:T(8,128)(2,1)} async-done(((bf16[1,24,512]{2,1,0:T(8,128)(2,1)}), bf16[1,1536,512]{2,1,0:T(8,128)(2,1)}) %all-gather.16.cloned.1.call-update) | async-done | bytes 1572880 | tf_op jit(solution)/shard_map/all_gather | solution.py:77
  351.0 6.4 %fusion.56 = (f32[1024]{0:T(1024)S(1)}, f32[1024,512]{1,0:T(8,128)S(1)}) fusion(bf16[1,1536,512]{2,1,0:T(8,128)(2,1)} %all-gather.16.cloned.1.call-done, bf16[1,1024,512]{2,1,0:T(8,128)(2,1)S(1)} %bitcast.99, bf16[1,8,512]{2,1,0:T(8,128)(2,1)S(1)} %slice.129, bf16[1,1024,512]{2,1,0:T(8,128)(2,1)} %fusion.34), kind=kOutput, calls=%fused_computation.105 | convolution fusion | flops 1623718912 | bytes 5779456 | tf_op jit(solution)/shard_map/dot_general | solution.py:75
  360.3 73.4 %all-gather.18.cloned.1.call-done = bf16[1,1536,512]{2,1,0:T(8,128)(2,1)} async-done(((bf16[1,24,512]{2,1,0:T(8,128)(2,1)}), bf16[1,1536,512]{2,1,0:T(8,128)(2,1)}) %all-gather.18.cloned.1.call-update) | async-done | bytes 1572880 | tf_op jit(solution)/shard_map/all_gather | solution.py:77
  433.7 5.5 %fusion.57 = (f32[1024]{0:T(1024)S(1)}, f32[1024,512]{0,1:T(8,128)}) fusion(bf16[1,1536,512]{2,1,0:T(8,128)(2,1)} %all-gather.18.cloned.1.call-done, bf16[1,1024,512]{2,1,0:T(8,128)(2,1)} %copy-done.3, bf16[1,16,512]{2,1,0:T(8,128)(2,1)S(1)} %slice.132, bf16[1,1024,512]{2,1,0:T(8,128)(2,1)} %fusion.36), kind=kOutput, calls=%fused_computation.106 | convolution fusion | flops 1623718912 | bytes 5787648 | tf_op jit(solution)/shard_map/dot_general | solution.py:75
  439.3 2.9 copy.27
  442.2 2.1 multiply_reduce_fusion
  444.4 1.5 fusion.39
  (84 shorter events, 21.5 us)
Async XLA Ops:
  6.5 113.4 %copy-start = (bf16[4,2048,128]{2,1,0:T(8,128)(2,1)S(1)}, bf16[4,2048,128]{2,1,0:T(8,128)(2,1)}, u32[]{:S(2)}) copy-start(bf16[4,2048,128]{2,1,0:T(8,128)(2,1)} %param.14) | copy-start | bytes 6291460
  6.5 4.4 copy-start.6
  6.5 165.6 %all-gather.10.cloned.1.call-start = ((), (), s32[]{:S(2)}) async-start(), calls=%async_computation.2 | async-start | bytes 2211840 | tf_op jit(solution)/shard_map/all_gather | solution.py:66
  7.3 278.6 %all-gather.12.cloned.1.call-start = ((), (), s32[]{:S(2)}) async-start(), calls=%async_computation.3 | async-start | bytes 1597440 | tf_op jit(solution)/shard_map/all_gather | solution.py:77
  8.8 283.3 %all-gather.14.cloned.1.call-start = ((), (), s32[]{:S(2)}) async-start(), calls=%async_computation.4 | async-start | bytes 1597440 | tf_op jit(solution)/shard_map/all_gather | solution.py:77
  55.4 4.1 copy-start.8
  55.4 4.1 copy-start.10
  163.3 8.8 %copy-start.9 = (f32[4,512]{1,0:T(4,128)S(1)}, f32[4,512]{1,0:T(4,128)}, u32[]{:S(2)}) copy-start(f32[4,512]{1,0:T(4,128)} %param.20) | copy-start | bytes 24580
  163.3 81.7 %all-to-all-start.1 = ((bf16[64,192,128]{2,1,0:T(8,128)(2,1)}), bf16[64,192,128]{2,1,0:T(8,128)(2,1)}, u32[]{:S(2)}, u32[]{:S(2)}) async-start(bf16[64,192,128]{2,1,0:T(8,128)(2,1)} %bitcast.97), calls=%async_computation.1 | async-start | bytes 6291456 | tf_op jit(solution)/shard_map/all_to_all | solution.py:58
  169.0 182.1 %all-gather.16.cloned.1.call-start = ((), (), s32[]{:S(2)}) async-start(), calls=%async_computation.5 | async-start | bytes 1597440 | tf_op jit(solution)/shard_map/all_gather | solution.py:77
  169.6 264.2 %all-gather.18.cloned.1.call-start = ((), (), s32[]{:S(2)}) async-start(), calls=%async_computation.6 | async-start | bytes 1597440 | tf_op jit(solution)/shard_map/all_gather | solution.py:77
  275.5 1.9 copy-start.7
  278.5 2.0 copy-start.2
  279.6 5.1 %copy-start.4 = (bf16[1024,128]{1,0:T(8,128)(2,1)}, bf16[1024,128]{1,0:T(8,128)(2,1)S(1)}, u32[]{:S(2)}) copy-start(bf16[1024,128]{1,0:T(8,128)(2,1)S(1)} %slice_reduce_fusion) | copy-start | bytes 786436
  295.8 1.7 copy-start.5
  358.3 1.0 copy-start.3
  442.2 2.2 copy-start.1
Sparse Core Ops, SparseCore 0:
  9.5 33.5 all-gather.9
  46.1 84.5 all-gather.11
  133.7 134.6 all-gather.13
  271.2 79.7 all-gather.15
  353.9 79.7 all-gather.17
where the time goes:
time: 457 us; the launch traced here: 452 us
  waiting for transfers between devices  199 us (44%)
  local copies, waits for them, and re-layouts  125 us (27%)
  other arithmetic  58.5 us (13%)
  blocking collectives  29.1 us (6%)
  matrix products  19.9 us (4%)
  between operations  15.5 us (3%)
  starting transfers between devices  5.88 us (1%)
    all_gather x4, waiting for transfers between devices, local(): lax.all_gather(conv_weight[layer], 'table', axis=0, tiled=True)  125 us
    all_to_all x1, waiting for transfers between devices, local(): lax.all_to_all(flat_table[received], 'table', split_axis=0, concat_axis=0...  71.7 us
    gather x1, local copies, waits for them, and re-layouts, local(): flat_table[received]  43.3 us
    another operation x3, other arithmetic  39.5 us
    gather x1, local copies, waits for them, and re-layouts, local(): returned.reshape(owners * capacity, row_width)[placed].astype(jnp.float32)  30.5 us
    scatter x1, local copies, waits for them, and re-layouts, local(): requests = jnp.zeros((owners * capacity,), jnp.int32).at[placed].set(loca...  30.5 us
    all_to_all x1, blocking collectives, local(): lax.all_to_all(requests, 'table', split_axis=0, concat_axis=0, tiled=True)  29.1 us
    dot_general x4, matrix products, local(): jnp.dot(stacked, lax.all_gather(conv_weight[layer], 'table', axis=0, tile...  19.9 us
  transfers between devices with their start and end apart: 6, of which 3 were waited for; matrix products, arithmetic and copies ran while one was open for 42% of the time, Pallas kernels for 0%

commit v1 on v0

v1 whole, which is shorter than its diff:
```python
import functools

import jax
import jax.numpy as jnp
from jax import lax
from jax.experimental import pallas as pl
from jax.experimental.pallas import tpu as pltpu
from jax.sharding import PartitionSpec as P

table_of_id = (0, 1, 2, 2, 3, 3, 3, 3)
epsilon = 1e-05
MESH = pl.DeviceIdType.MESH
MIB = 1024 * 1024


def whole(memory=pltpu.VMEM):
    return pl.BlockSpec(memory_space=memory)


def split_index(index):
    return lax.rem(index * 27, 64)


def route_kernel(shard_rows, capacity, owner_ref, rows_ref, req_ref, placed_ref, mem_ref, run_ref):
    slots, bag = owner_ref.shape
    owners = req_ref.shape[0]
    step = 128
    f32, bf16 = jnp.float32, jnp.bfloat16
    lane = lax.broadcasted_iota(jnp.int32, (slots, 128), 1)
    upper = lane >= owners
    lane_owner = jnp.where(upper, lane - owners, lane)
    owned = owner_ref[...]
    local_rows = rows_ref[...]
    named = jnp.zeros((slots, 128), f32)
    for k in range(bag):
        named = named + jnp.where(owned[:, k : k + 1] == lane_owner, 1.0, 0.0)
    mem_ref[...] = named.astype(bf16)
    below = (
        lax.broadcasted_iota(jnp.int32, (step, step), 1)
        < lax.broadcasted_iota(jnp.int32, (step, step), 0)
    ).astype(f32).astype(bf16)
    total = jnp.zeros((1, 128), f32)
    for part in range(slots // step):
        block = mem_ref[part * step : (part + 1) * step, :]
        run_ref[part * step : (part + 1) * step, :] = total + jnp.dot(
            below, block, preferred_element_type=f32
        )
        total = total + jnp.sum(block.astype(f32), axis=0, keepdims=True)
    ranks = run_ref[...]
    spread = (
        (lax.broadcasted_iota(jnp.int32, (128, 256), 0) < owners).astype(f32).astype(bf16)
    )
    column = lax.broadcasted_iota(jnp.int32, (slots, 256), 1).astype(f32)
    pick_row = lax.broadcasted_iota(jnp.int32, (16, 128), 0)
    pick_upper = lax.broadcasted_iota(jnp.int32, (16, 128), 1) >= owners
    requests = jnp.zeros((128, 256), f32)
    places = jnp.zeros((16, slots), f32)
    for k in range(bag):
        hit = owned[:, k : k + 1] == lane_owner
        value = local_rows[:, k : k + 1] + table_of_id[k] * shard_rows
        parts = jnp.where(upper, value & 63, value >> 6)
        words = jnp.where(hit, parts, 0).astype(f32).astype(bf16)
        marks = jnp.where(hit, jnp.where(upper, lane_owner.astype(f32), ranks), 0.0).astype(bf16)
        rank_wide = jnp.dot(marks, spread, preferred_element_type=f32)
        places_here = jnp.where(rank_wide == column, 1.0, 0.0).astype(bf16)
        requests = requests + lax.dot_general(
            words, places_here, (((0,), (0,)), ((), ())), preferred_element_type=f32
        )
        pick = (
            (pick_row == jnp.where(pick_upper, 8 + k, k)).astype(f32).astype(bf16)
        )
        places = places + lax.dot_general(
            pick, marks, (((1,), (1,)), ((), ())), preferred_element_type=f32
        )
    req_ref[...] = (requests[:owners] * 64.0 + requests[owners : 2 * owners]).astype(jnp.int32)
    placed_ref[...] = (places[8:16] * float(capacity) + places[0:8]).astype(jnp.int32)


def exchange_kernel(
    capacity,
    req_ref,
    entry_ref,
    table_ref,
    stores_ref,
    rows_out,
    carried_out,
    wide_table,
    stage,
    send_rows,
    req_in,
    req_words,
    entry_in,
    entry_words,
    send_state,
    req_send,
    req_recv,
    row_send,
    row_recv,
    entry_send,
    entry_recv,
    state_send,
    state_recv,
    local_sem,
):
    owners = req_ref.shape[0]
    peers = entry_in.shape[0]
    side = 8
    me = lax.axis_index("table")
    rep = lax.axis_index("rep")
    my_z, my_y = me // side, lax.rem(me, side)

    def partner(index):
        offset = split_index(index)
        return lax.rem(my_z + offset // side, side) * side + lax.rem(my_y + lax.rem(offset, side), side)

    def origin(index):
        offset = split_index(index)
        return (
            lax.rem(my_z + side - offset // side, side) * side
            + lax.rem(my_y + side - lax.rem(offset, side), side)
        )

    barrier = pltpu.get_barrier_semaphore()

    @pl.loop(1, owners)
    def _(i):
        pl.semaphore_signal(barrier, inc=1, device_id=(partner(i), rep), device_id_type=MESH)

    @pl.loop(1, peers)
    def _(i):
        pl.semaphore_signal(
            barrier, inc=1, device_id=(me, lax.rem(rep + i, peers)), device_id_type=MESH
        )

    pl.semaphore_wait(barrier, owners - 1 + peers - 1)

    def request_copy(index):
        to = partner(index)
        return pltpu.make_async_remote_copy(
            src_ref=req_ref.at[pl.ds(to, 1)],
            dst_ref=req_in.at[pl.ds(me, 1)],
            send_sem=req_send.at[to],
            recv_sem=req_recv.at[me],
            device_id=(to, rep),
            device_id_type=MESH,
        )

    def request_arrival(index):
        source = origin(index)
        return pltpu.make_async_remote_copy(
            src_ref=req_ref.at[pl.ds(source, 1)],
            dst_ref=req_in.at[pl.ds(source, 1)],
            send_sem=req_send.at[source],
            recv_sem=req_recv.at[source],
            device_id=(source, rep),
            device_id_type=MESH,
        )

    def entry_copy(index):
        to = lax.rem(rep + index, peers)
        return pltpu.make_async_remote_copy(
            src_ref=entry_ref,
            dst_ref=entry_in.at[pl.ds(rep, 1)],
            send_sem=entry_send.at[to],
            recv_sem=entry_recv.at[rep],
            device_id=(me, to),
            device_id_type=MESH,
        )

    def entry_arrival(index):
        source = lax.rem(rep + peers - index, peers)
        return pltpu.make_async_remote_copy(
            src_ref=entry_ref,
            dst_ref=entry_in.at[pl.ds(source, 1)],
            send_sem=entry_send.at[source],
            recv_sem=entry_recv.at[source],
            device_id=(me, source),
            device_id_type=MESH,
        )

    def state_copy(index):
        to = lax.rem(rep + index, peers)
        return pltpu.make_async_remote_copy(
            src_ref=send_state.at[to],
            dst_ref=carried_out.at[rep],
            send_sem=state_send.at[to],
            recv_sem=state_recv.at[rep],
            device_id=(me, to),
            device_id_type=MESH,
        )

    def state_arrival(index):
        source = lax.rem(rep + peers - index, peers)
        return pltpu.make_async_remote_copy(
            src_ref=send_state.at[source],
            dst_ref=carried_out.at[source],
            send_sem=state_send.at[source],
            recv_sem=state_recv.at[source],
            device_id=(me, source),
            device_id_type=MESH,
        )

    def row_copy(index):
        to = partner(index)
        return pltpu.make_async_remote_copy(
            src_ref=send_rows.at[to],
            dst_ref=rows_out.at[me],
            send_sem=row_send.at[to],
            recv_sem=row_recv.at[me],
            device_id=(to, rep),
            device_id_type=MESH,
        )

    def row_arrival(index):
        source = origin(index)
        return pltpu.make_async_remote_copy(
            src_ref=send_rows.at[source],
            dst_ref=rows_out.at[source],
            send_sem=row_send.at[source],
            recv_sem=row_recv.at[source],
            device_id=(source, rep),
            device_id_type=MESH,
        )

    @pl.loop(1, owners)
    def _(i):
        request_copy(i).start()

    @pl.loop(1, peers)
    def _(i):
        entry_copy(i).start()

    req_in[pl.ds(me, 1), :] = req_ref[pl.ds(me, 1), :]
    entry_in[pl.ds(rep, 1), :] = entry_ref[...]

    tile = 256

    @pl.loop(0, table_ref.shape[0] // tile)
    def _(i):
        at = pl.multiple_of(i * tile, tile)
        wide_table[pl.ds(at, tile), :] = table_ref[pl.ds(at, tile), :].astype(jnp.float32)

    @pl.loop(1, peers)
    def _(i):
        entry_arrival(i).wait_recv()

    entry_move = pltpu.make_async_copy(entry_in, entry_words, local_sem.at[0])
    entry_move.start()
    entry_move.wait()

    @pl.loop(0, peers)
    def _(i):
        to = lax.rem(rep + i, peers)
        send_state[to] = stores_ref[entry_words[to, 0]]

    @pl.loop(1, peers)
    def _(i):
        state_copy(i).start()

    own_state = pltpu.make_async_copy(send_state.at[rep], carried_out.at[rep], local_sem.at[1])
    own_state.start()

    @pl.loop(1, owners)
    def _(i):
        request_arrival(i).wait_recv()

    req_move = pltpu.make_async_copy(req_in, req_words, local_sem.at[0])
    req_move.start()
    req_move.wait()

    def gather(to):
        @pl.loop(0, capacity // 16)
        def _(c):
            for u in range(16):
                row = req_words[to, c * 16 + u]
                stage[pl.ds(c * 16 + u, 1), :] = wide_table[pl.ds(row, 1), :]

        send_rows[to] = stage[...].astype(jnp.bfloat16)

    @pl.loop(1, owners)
    def _(i):
        gather(partner(i))
        row_copy(i).start()

    gather(me)
    own_rows = pltpu.make_async_copy(send_rows.at[me], rows_out.at[me], local_sem.at[0])
    own_rows.start()
    own_rows.wait()
    own_state.wait()

    @pl.loop(1, owners)
    def _(i):
        request_copy(i).wait_send()

    @pl.loop(1, peers)
    def _(i):
        entry_copy(i).wait_send()
        state_copy(i).wait_send()
        state_arrival(i).wait_recv()

    @pl.loop(1, owners)
    def _(i):
        row_copy(i).wait_send()
        row_arrival(i).wait_recv()


def convolve_kernel(
    rows_ref,
    placed_ref,
    weight_ref,
    where_ref,
    carried_ref,
    filters_ref,
    gain_ref,
    out_ref,
    wide_rows,
    stage,
    even_in,
    odd_in,
):
    f32, bf16 = jnp.float32, jnp.bfloat16
    slots, bag = weight_ref.shape
    width = rows_ref.shape[1]
    channels = out_ref.shape[1]
    layers = filters_ref.shape[0]
    head = even_in.shape[0] - slots
    tile = 512

    @pl.loop(0, rows_ref.shape[0] // tile)
    def _(i):
        at = pl.multiple_of(i * tile, tile)
        wide_rows[pl.ds(at, tile), :] = rows_ref[pl.ds(at, tile), :].astype(f32)

    @pl.loop(0, slots // 8)
    def _(i):
        base = pl.multiple_of(i * 8, 8)
        for k in range(bag):
            for j in range(8):
                stage[k * 8 + j : k * 8 + j + 1, :] = wide_rows[
                    pl.ds(placed_ref[k, base + j], 1), :
                ]
        weights = weight_ref[pl.ds(base, 8), :]
        terms = [stage[k * 8 : k * 8 + 8, :] * weights[:, k : k + 1] for k in range(bag)]
        sums = (
            terms[0],
            terms[1],
            terms[2] + terms[3],
            (terms[4] + terms[5]) + (terms[6] + terms[7]),
        )
        for t in range(4):
            even_in[pl.ds(head + base, 8), t * width : (t + 1) * width] = (
                sums[t].astype(bf16).astype(f32)
            )

    state = carried_ref[where_ref[0]].astype(f32)
    state = jnp.where(where_ref[1] > 0, state, 0.0)
    block = 256
    offset = 0
    for layer in range(layers):
        dilation = 2**layer
        span = 2 * dilation
        source, target = (even_in, odd_in) if layer % 2 == 0 else (odd_in, even_in)
        source[head - span : head, :] = state[offset : offset + span, :]
        offset = offset + span
        for part in range(slots // block):
            low = head + part * block
            taps = [
                source[low - tap * dilation : low - tap * dilation + block, :].astype(bf16)
                for tap in range(3)
            ]
            values = jnp.dot(
                jnp.concatenate(taps, axis=1), filters_ref[layer], preferred_element_type=f32
            )
            mean = jnp.mean(values, axis=-1, keepdims=True)
            centred = values - mean
            spread = jnp.mean(centred * centred, axis=-1, keepdims=True)
            active = jnp.maximum(
                centred * lax.rsqrt(spread + epsilon) * gain_ref[layer : layer + 1, :], 0.0
            )
            if layer % 2 == 1:
                active = active + target[low : low + block, :]
            if layer == layers - 1:
                out_ref[part * block : (part + 1) * block, :] = active.astype(bf16)
            else:
                target[low : low + block, :] = active.astype(bf16).astype(f32)


def local(
    bag_rows, bag_owner, bag_weight, tables, returning, home, entry, stores, conv_weight, norm_gain
):
    i32, f32, bf16 = jnp.int32, jnp.float32, jnp.bfloat16
    owners = lax.axis_size("table")
    peers = lax.axis_size("rep")
    slots, bag = bag_rows.shape[1:]
    shard_rows, width = tables.shape[1:]
    layers, _, channels = conv_weight.shape
    capacity = min(slots, (3 * slots * bag + 2 * owners - 1) // (2 * owners))
    entries, state_len = stores.shape[:2]
    state_rows = 32

    filters = lax.all_gather(conv_weight, "table", axis=1, tiled=True)

    requests, placed = pl.pallas_call(
        functools.partial(route_kernel, shard_rows, capacity),
        out_shape=(
            jax.ShapeDtypeStruct((owners, 256), i32),
            jax.ShapeDtypeStruct((bag, slots), i32),
        ),
        in_specs=[whole(), whole()],
        out_specs=(whole(), whole()),
        scratch_shapes=[pltpu.VMEM((slots, 128), bf16), pltpu.VMEM((slots, 128), f32)],
        compiler_params=pltpu.CompilerParams(vmem_limit_bytes=40 * MIB),
        name="route",
    )(bag_owner[0], bag_rows[0])

    padded = jnp.pad(stores, ((0, 0), (0, state_rows - state_len), (0, 0)))
    rows, carried = pl.pallas_call(
        functools.partial(exchange_kernel, capacity),
        out_shape=(
            jax.ShapeDtypeStruct((owners, capacity, width), bf16),
            jax.ShapeDtypeStruct((peers, state_rows, channels), bf16),
        ),
        in_specs=[whole(), whole(), whole(), whole()],
        out_specs=(whole(pl.ANY), whole(pl.ANY)),
        scratch_shapes=[
            pltpu.VMEM((4 * shard_rows, width), f32),
            pltpu.VMEM((capacity, width), f32),
            pltpu.VMEM((owners, capacity, width), bf16),
            pltpu.VMEM((owners, 256), i32),
            pltpu.SMEM((owners, 256), i32),
            pltpu.VMEM((peers, 128), i32),
            pltpu.SMEM((peers, 128), i32),
            pltpu.VMEM((peers, state_rows, channels), bf16),
            pltpu.SemaphoreType.DMA((owners,)),
            pltpu.SemaphoreType.DMA((owners,)),
            pltpu.SemaphoreType.DMA((owners,)),
            pltpu.SemaphoreType.DMA((owners,)),
            pltpu.SemaphoreType.DMA((peers,)),
            pltpu.SemaphoreType.DMA((peers,)),
            pltpu.SemaphoreType.DMA((peers,)),
            pltpu.SemaphoreType.DMA((peers,)),
            pltpu.SemaphoreType.DMA((2,)),
        ],
        compiler_params=pltpu.CompilerParams(
            collective_id=0, has_side_effects=True, vmem_limit_bytes=40 * MIB
        ),
        name="exchange",
    )(
        requests,
        jnp.broadcast_to(entry[:, None], (1, 128)),
        tables.reshape(4 * shard_rows, width),
        padded,
    )

    hidden = pl.pallas_call(
        convolve_kernel,
        out_shape=jax.ShapeDtypeStruct((slots, channels), bf16),
        in_specs=[
            whole(),
            whole(pltpu.SMEM),
            whole(),
            whole(pltpu.SMEM),
            whole(),
            whole(),
            whole(),
        ],
        out_specs=whole(),
        scratch_shapes=[
            pltpu.VMEM((owners * capacity, width), f32),
            pltpu.VMEM((8 * bag, width), f32),
            pltpu.VMEM((32 + slots, channels), f32),
            pltpu.VMEM((32 + slots, channels), f32),
        ],
        compiler_params=pltpu.CompilerParams(vmem_limit_bytes=48 * MIB),
        name="convolve",
    )(
        rows.reshape(owners * capacity, width),
        placed,
        bag_weight[0],
        jnp.concatenate([home, returning]),
        carried,
        filters,
        norm_gain,
    )
    return hidden[None]


def solution(mesh):
    in_specs = (
        P(("table", "rep"), None, None),
        P(("table", "rep"), None, None),
        P(("table", "rep"), None, None),
        P(None, "table", None),
        P(("table", "rep")),
        P(("table", "rep")),
        P(("table", "rep")),
        P(("table", "rep"), None, None),
        P(None, "table", None),
        P(),
    )
    out_specs = P(("table", "rep"), None, None)
    return jax.shard_map(local, mesh=mesh, in_specs=in_specs, out_specs=out_specs, check_vma=False)
```

time: 457 us -> 199 us (0.44)
  waiting for transfers between devices: 199 us -> 40.6 us
  Pallas kernels: 0 us -> 135 us
  local copies, waits for them, and re-layouts: 125 us -> 7.35 us
  other arithmetic: 58.5 us -> 0.08 us
  blocking collectives: 29.1 us -> 0 us
  matrix products: 19.9 us -> 0 us
  starting transfers between devices: 5.88 us -> 0.01 us
    pallas_call x0 -> x3, Pallas kernels: none -> 135 us  [the longest x1 106 us: local(): pl.pallas_call(functools.partial(exchange_kernel, capacity), out_shape=(j...]
    all_gather x5 -> x1, waiting for transfers between devices: 125 us -> 39.9 us  [local(): filters = lax.all_gather(conv_weight, 'table', axis=1, tiled=True)]
    gather x3 -> x0, local copies, waits for them, and re-layouts: 74.8 us -> none  [the longest x1 43.3 us: local(): flat_table[received]]
    all_to_all x1 -> x0, waiting for transfers between devices: 71.7 us -> none  [local(): lax.all_to_all(flat_table[received], 'table', split_axis=0, concat_axis=0...]
    another operation x3 -> x0, other arithmetic: 39.5 us -> none
    scatter x1 -> x0, local copies, waits for them, and re-layouts: 30.5 us -> none  [local(): requests = jnp.zeros((owners * capacity,), jnp.int32).at[placed].set(loca...]
    all_to_all x1 -> x0, blocking collectives: 29.1 us -> none  [local(): lax.all_to_all(requests, 'table', split_axis=0, concat_axis=0, tiled=True)]
    dot_general x4 -> x0, matrix products: 19.9 us -> none  [local(): jnp.dot(stacked, lax.all_gather(conv_weight[layer], 'table', axis=0, tile...]
  transfers between devices with their start and end apart: 6 -> 1, of which waited for: 3 -> 1; matrix products, arithmetic and copies ran while one was open for 42% -> 2% of each run, Pallas kernels for 0% -> 56%
where the time goes in v1:
time: 199 us; the launch traced here: 198 us
  Pallas kernels  135 us (68%)
  waiting for transfers between devices  40.6 us (20%)
  between operations  15.4 us (8%)
  local copies, waits for them, and re-layouts  7.35 us (4%)
    pallas_call x1, Pallas kernels, local(): pl.pallas_call(functools.partial(exchange_kernel, capacity), out_shape=(j...  106 us
    all_gather x1, waiting for transfers between devices, local(): filters = lax.all_gather(conv_weight, 'table', axis=1, tiled=True)  39.9 us
    pallas_call x1, Pallas kernels, local(): pl.pallas_call(convolve_kernel, out_shape=jax.ShapeDtypeStruct((slots, ch...  23.9 us
    unnamed x10, local copies, waits for them, and re-layouts  7.32 us
    pallas_call x1, Pallas kernels, local(): pl.pallas_call(functools.partial(route_kernel, shard_rows, capacity), out...  4.75 us
  transfers between devices with their start and end apart: 1, of which 1 were waited for; matrix products, arithmetic and copies ran while one was open for 2% of the time, Pallas kernels for 56%

profile of v1, /device:TPU:6, one launch (start us, length us, event | category | flops | bytes accessed | tf_op | source)
XLA Modules:
  0.0 198.0 jit_solution(9081533387698730843)
XLA Ops:
  6.5 0.0 copy-start.2
  6.5 0.0 all-gather.2.cloned.1.call-start
  6.5 0.7 all-gather.2.cloned.1.call-update
  9.2 1.0 copy.13
  10.2 1.0 copy.12
  11.2 1.0 copy.11
  12.1 1.8 copy.14
  13.9 4.8 %route.1 = (s32[64,256]{1,0:T(8,128)S(1)}, s32[8,1024]{1,0:T(8,128)S(1)}) custom-call(s32[1024,8]{1,0:T(8,128)S(1)} %bitcast.12, s32[1024,8]{1,0:T(8,128)S(1)} %bitcast.11), custom_call_target="tpu_custom_call" | custom-call | tf_op jit(solution)/shard_map/route/pallas_call | solution.py:403
  18.7 0.0 copy-start.1
  18.7 1.6 copy-done.1
  20.3 106.0 %exchange.1 = (bf16[64,192,128]{2,1,0:T(8,128)(2,1)S(1)}, bf16[8,32,512]{2,1,0:T(8,128)(2,1)S(1)}) custom-call(s32[64,256]{1,0:T(8,128)S(1)} %get-tuple-element.9.req_ref, s32[1,128]{1,0:T(1,128)S(1)} %broadcast_in_dim.12.entry_ref, bf16[8192,128]{1,0:T(8,128)(2,1)S(1)} %bitcast.10, bf16[8,32,512]{2,1,0:T(8,128)(2,1)S(1)} %pad.4.stores_ref), custom_call_target="tpu_custom_call" | custom-call | tf_op jit(solution)/shard_map/exchange/pallas_call | solution.py:417
  126.3 0.1 pad_add_fusion.where_ref
  126.4 39.9 %all-gather.2.cloned.1.call-done.filters_ref = bf16[4,1536,512]{2,1,0:T(8,128)(2,1)} async-done(((bf16[4,24,512]{2,1,0:T(8,128)(2,1)}), bf16[4,1536,512]{2,1,0:T(8,128)(2,1)}) %all-gather.2.cloned.1.call-update) | async-done | bytes 6291472 | tf_op jit(solution)/shard_map/all_gather | solution.py:401
  166.2 0.0 copy-done.2
  166.2 0.0 copy-start
  166.2 1.0 copy-done
  167.3 23.9 %convolve.1 = bf16[1024,512]{1,0:T(8,128)(2,1)} custom-call(bf16[12288,128]{1,0:T(8,128)(2,1)S(1)} %bitcast.8, s32[8,1024]{1,0:T(8,128)S(1)} %get-tuple-element.11.placed_ref, f32[1024,8]{1,0:T(8,128)S(1)} %bitcast.9, s32[2]{0:T(128)S(1)} %pad_add_fusion.where_ref, bf16[8,32,512]{2,1,0:T(8,128)(2,1)S(1)} %get-tuple-element.12.carried_ref, ...), custom_call_target="tpu_custom_call" | custom-call | tf_op jit(solution)/shard_map/convolve/pallas_call | solution.py:455
  (2 shorter events, 0.0 us)
Async XLA Ops:
  6.5 159.7 %copy-start.2 = (f32[4,512]{1,0:T(4,128)S(1)}, f32[4,512]{1,0:T(4,128)}, u32[]{:S(2)}) copy-start(f32[4,512]{1,0:T(4,128)} %gain_ref.1) | copy-start | bytes 24580
  6.5 159.7 %all-gather.2.cloned.1.call-start = ((), (), s32[]{:S(2)}) async-start(), calls=%async_computation | async-start | bytes 6389760 | tf_op jit(solution)/shard_map/all_gather | solution.py:401
  18.7 1.6 copy-start.1
  166.2 1.0 copy-start
Sparse Core Ops, SparseCore 0:
  10.4 155.8 all-gather.1

commit v2 on v1

v2 whole, which is shorter than its diff:
```python
import functools

import jax
import jax.numpy as jnp
from jax import lax
from jax.experimental import pallas as pl
from jax.experimental.pallas import tpu as pltpu
from jax.sharding import PartitionSpec as P

table_of_id = (0, 1, 2, 2, 3, 3, 3, 3)
epsilon = 1e-05
MESH = pl.DeviceIdType.MESH
MIB = 1024 * 1024


def whole(memory=pltpu.VMEM):
    return pl.BlockSpec(memory_space=memory)


def split_index(index):
    return lax.rem(index * 27, 64)


def route(shard_rows, capacity, owner_ref, rows_ref, req_ref, placed_ref):
    bag, slots = owner_ref.shape
    owners, columns = req_ref.shape
    step = 256
    f32, bf16 = jnp.float32, jnp.bfloat16
    owner_row = lax.broadcasted_iota(jnp.int32, (owners, slots), 0)
    named = jnp.zeros((owners, slots), f32)
    for k in range(bag):
        named = named + jnp.where(owner_ref[k : k + 1, :] == owner_row, 1.0, 0.0)
    before = (
        lax.broadcasted_iota(jnp.int32, (step, step), 0)
        < lax.broadcasted_iota(jnp.int32, (step, step), 1)
    ).astype(f32).astype(bf16)
    total = jnp.zeros((owners, 1), f32)
    ranked = []
    for part in range(slots // step):
        block = named[:, part * step : (part + 1) * step]
        ranked.append(total + jnp.dot(block.astype(bf16), before, preferred_element_type=f32))
        total = total + jnp.sum(block, axis=1, keepdims=True)
    ranks = jnp.concatenate(ranked, axis=1)
    place_row = lax.broadcasted_iota(jnp.int32, (columns, slots), 0)
    requests = jnp.zeros((2 * owners, columns), f32)
    for k in range(bag):
        owner = owner_ref[k : k + 1, :]
        hit = owner == owner_row
        rank = jnp.sum(jnp.where(hit, ranks, 0.0), axis=0, keepdims=True).astype(jnp.int32)
        placed_ref[k : k + 1, :] = owner * capacity + rank
        value = rows_ref[k : k + 1, :] + table_of_id[k] * shard_rows
        high = jnp.where(hit, (value >> 6).astype(f32), 0.0)
        low = jnp.where(hit, (value & 63).astype(f32), 0.0)
        words = jnp.concatenate([high, low], axis=0).astype(bf16)
        marks = jnp.where(place_row == rank, 1.0, 0.0).astype(bf16)
        requests = requests + lax.dot_general(
            words, marks, (((1,), (1,)), ((), ())), preferred_element_type=f32
        )
    wanted = (requests[:owners] * 64.0 + requests[owners:]).astype(jnp.int32)
    req_ref[...] = jnp.clip(wanted, 0, 4 * shard_rows - 1)


def exchange_kernel(
    shard_rows,
    capacity,
    owner_ref,
    bag_rows_ref,
    entry_ref,
    table_ref,
    stores_ref,
    shard_ref,
    placed_out,
    rows_out,
    carried_out,
    filters_out,
    table_here,
    stores_here,
    wide_table,
    wide_stores,
    state_stage,
    stage,
    send_rows,
    req_ref,
    req_in,
    req_words,
    entry_in,
    entry_words,
    send_state,
    pieces,
    gathered,
    req_send,
    req_recv,
    row_send,
    row_recv,
    entry_send,
    entry_recv,
    state_send,
    state_recv,
    near_send,
    near_recv,
    far_send,
    far_recv,
    line_send,
    line_recv,
    core_send,
    core_recv,
    local_sem,
):
    owners = req_ref.shape[0]
    peers = entry_in.shape[0]
    side = 8
    me = lax.axis_index("table")
    rep = lax.axis_index("rep")
    my_z, my_y = me // side, lax.rem(me, side)

    def partner(index):
        offset = split_index(index)
        return lax.rem(my_z + offset // side, side) * side + lax.rem(my_y + lax.rem(offset, side), side)

    def origin(index):
        offset = split_index(index)
        return (
            lax.rem(my_z + side - offset // side, side) * side
            + lax.rem(my_y + side - lax.rem(offset, side), side)
        )

    def remote(source, target, sender, receiver, table, line):
        return pltpu.make_async_remote_copy(
            src_ref=source,
            dst_ref=target,
            send_sem=sender,
            recv_sem=receiver,
            device_id=(table, line),
            device_id_type=MESH,
        )

    def request_copy(index):
        to = partner(index)
        return remote(
            req_ref.at[pl.ds(to, 1)], req_in.at[pl.ds(me, 1)], req_send.at[to], req_recv.at[me], to, rep
        )

    def request_arrival(index):
        source = origin(index)
        block = req_in.at[pl.ds(source, 1)]
        return remote(block, block, req_send.at[source], req_recv.at[source], source, rep)

    def entry_copy(index):
        to = lax.rem(rep + index, peers)
        return remote(
            entry_ref, entry_in.at[pl.ds(rep, 1)], entry_send.at[to], entry_recv.at[rep], me, to
        )

    def entry_arrival(index):
        source = lax.rem(rep + peers - index, peers)
        block = entry_in.at[pl.ds(source, 1)]
        return remote(block, block, entry_send.at[source], entry_recv.at[source], me, source)

    def state_copy(index):
        to = lax.rem(rep + index, peers)
        return remote(
            send_state.at[to], carried_out.at[rep], state_send.at[to], state_recv.at[rep], me, to
        )

    def state_arrival(index):
        source = lax.rem(rep + peers - index, peers)
        block = carried_out.at[source]
        return remote(block, block, state_send.at[source], state_recv.at[source], me, source)

    def row_copy(index):
        to = partner(index)
        return remote(send_rows.at[to], rows_out.at[me], row_send.at[to], row_recv.at[me], to, rep)

    def row_arrival(index):
        source = origin(index)
        block = rows_out.at[source]
        return remote(block, block, row_send.at[source], row_recv.at[source], source, rep)

    core = lax.rem(rep, 2)
    spot = rep // 2
    other = rep + 1 - 2 * core
    spots = peers // 2
    major = my_z + core * (my_y - my_z)
    minor = my_y + core * (my_z - my_y)

    def at_plane(a, b):
        return a * (side - (side - 1) * core) + b * (1 + (side - 1) * core)

    def bundle(piece, a):
        return gathered.at[piece, pl.ds(a * side, side)]

    def near_copy(index):
        to = lax.rem(minor + index, side)
        return remote(
            pieces.at[rep],
            gathered.at[rep, major * side + minor],
            near_send.at[to],
            near_recv.at[minor],
            at_plane(major, to),
            rep,
        )

    def near_arrival(index):
        source = lax.rem(minor + side - index, side)
        block = gathered.at[rep, major * side + source]
        return remote(
            block, block, near_send.at[source], near_recv.at[source], at_plane(major, source), rep
        )

    def far_copy(index):
        to = lax.rem(major + index, side)
        return remote(
            bundle(rep, major),
            bundle(rep, major),
            far_send.at[to],
            far_recv.at[major],
            at_plane(to, minor),
            rep,
        )

    def far_arrival(index):
        source = lax.rem(major + side - index, side)
        block = bundle(rep, source)
        return remote(
            block, block, far_send.at[source], far_recv.at[source], at_plane(source, minor), rep
        )

    def line_copy(ahead, a):
        to = lax.rem(spot + ahead, spots)
        block = bundle(rep, a)
        return remote(block, block, line_send.at[to, a], line_recv.at[spot, a], me, to * 2 + core)

    def line_arrival(ahead, a):
        source = lax.rem(spot + spots - ahead, spots)
        block = bundle(source * 2 + core, a)
        return remote(
            block, block, line_send.at[source, a], line_recv.at[source, a], me, source * 2 + core
        )

    def core_copy(ahead, a):
        source = lax.rem(spot + spots - ahead, spots)
        block = bundle(source * 2 + core, a)
        return remote(block, block, core_send.at[source, a], core_recv.at[source, a], me, other)

    def core_arrival(ahead, a):
        source = lax.rem(spot + spots - ahead, spots)
        block = bundle(source * 2 + 1 - core, a)
        return remote(block, block, core_send.at[source, a], core_recv.at[source, a], me, other)

    barrier = pltpu.get_barrier_semaphore()

    @pl.loop(1, owners)
    def _(i):
        pl.semaphore_signal(barrier, inc=1, device_id=(partner(i), rep), device_id_type=MESH)

    @pl.loop(1, peers)
    def _(i):
        pl.semaphore_signal(
            barrier, inc=1, device_id=(me, lax.rem(rep + i, peers)), device_id_type=MESH
        )

    table_move = pltpu.make_async_copy(table_ref, table_here, local_sem.at[2])
    table_move.start()
    stores_move = pltpu.make_async_copy(stores_ref, stores_here, local_sem.at[3])
    stores_move.start()

    route(shard_rows, capacity, owner_ref, bag_rows_ref, req_ref, placed_out)

    half = shard_ref.shape[1]
    quarter = pieces.shape[2]
    for r in range(peers):
        lower, q = 2 * (r // 4), r % 4
        columns = slice(q * quarter, (q + 1) * quarter)
        pieces[r] = jnp.concatenate(
            [shard_ref[lower, :, columns], shard_ref[lower + 1, :, columns]], axis=0
        )

    pl.semaphore_wait(barrier, owners - 1 + peers - 1)

    @pl.loop(1, owners)
    def _(i):
        request_copy(i).start()

    @pl.loop(1, side)
    def _(i):
        near_copy(i).start()

    @pl.loop(1, peers)
    def _(i):
        entry_copy(i).start()

    req_in[pl.ds(me, 1), :] = req_ref[pl.ds(me, 1), :]
    entry_in[pl.ds(rep, 1), :] = entry_ref[...]
    gathered[rep, major * side + minor] = pieces[rep]

    tile = 256
    table_move.wait()

    @pl.loop(0, table_here.shape[0] // tile)
    def _(i):
        at = pl.multiple_of(i * tile, tile)
        wide_table[pl.ds(at, tile), :] = table_here[pl.ds(at, tile), :].astype(jnp.float32)

    @pl.loop(1, side)
    def _(i):
        near_arrival(i).wait_recv()

    @pl.loop(1, side)
    def _(i):
        far_copy(i).start()

    @pl.loop(1, owners)
    def _(i):
        request_arrival(i).wait_recv()

    req_move = pltpu.make_async_copy(req_in, req_words, local_sem.at[0])
    req_move.start()
    req_move.wait()

    def gather(to):
        for u in range(capacity):
            stage[u : u + 1, :] = wide_table[pl.ds(req_words[to, u], 1), :]
        send_rows[to] = stage[...].astype(jnp.bfloat16)

    @pl.loop(1, owners)
    def _(i):
        gather(partner(i))
        row_copy(i).start()

    @pl.loop(0, side)
    def _(i):
        a = lax.rem(major + side - i, side)

        @pl.when(i > 0)
        def _():
            far_arrival(i).wait_recv()

        for ahead in range(1, spots):
            line_copy(ahead, a).start()
        core_copy(0, a).start()

    gather(me)
    own_rows = pltpu.make_async_copy(send_rows.at[me], rows_out.at[me], local_sem.at[0])
    own_rows.start()

    stores_move.wait()
    wide_stores[...] = stores_here[...].astype(jnp.float32)
    state_stage[...] = jnp.zeros_like(state_stage)

    @pl.loop(1, peers)
    def _(i):
        entry_arrival(i).wait_recv()

    entry_move = pltpu.make_async_copy(entry_in, entry_words, local_sem.at[1])
    entry_move.start()
    entry_move.wait()

    @pl.loop(0, peers)
    def _(i):
        to = lax.rem(rep + i, peers)
        chosen = entry_words[to, 0]
        for row in range(stores_here.shape[0]):
            state_stage[row : row + 1, :] = wide_stores[row, pl.ds(chosen, 1), :]
        send_state[to] = state_stage[...].astype(jnp.bfloat16)

    @pl.loop(1, peers)
    def _(i):
        state_copy(i).start()

    own_state = pltpu.make_async_copy(send_state.at[rep], carried_out.at[rep], local_sem.at[1])
    own_state.start()

    @pl.loop(0, side)
    def _(i):
        a = lax.rem(major + side - i, side)
        for ahead in range(1, spots):
            line_arrival(ahead, a).wait_recv()
            core_copy(ahead, a).start()

    @pl.loop(0, side)
    def _(a):
        for ahead in range(spots):
            core_arrival(ahead, a).wait_recv()

    @pl.loop(0, owners // 2)
    def _(i):
        for r in range(peers):
            lower, q = 2 * (r // 4), r % 4
            columns = slice(q * quarter, (q + 1) * quarter)
            if r % 2 == 0:
                first, second = gathered[r, 2 * i], gathered[r, 2 * i + 1]
            else:
                slot = lax.rem(2 * i, side) * side + (2 * i) // side
                first, second = gathered[r, slot], gathered[r, slot + side]
            at = pl.multiple_of(i * 2 * half, 2 * half)
            filters_out[lower, pl.ds(at, 2 * half), columns] = jnp.concatenate(
                [first[:half], second[:half]], axis=0
            )
            filters_out[lower + 1, pl.ds(at, 2 * half), columns] = jnp.concatenate(
                [first[half:], second[half:]], axis=0
            )

    @pl.loop(1, side)
    def _(i):
        near_copy(i).wait_send()
        far_copy(i).wait_send()

    @pl.loop(0, side)
    def _(a):
        for ahead in range(1, spots):
            line_copy(ahead, a).wait_send()
        for ahead in range(spots):
            core_copy(ahead, a).wait_send()

    own_rows.wait()
    own_state.wait()

    @pl.loop(1, peers)
    def _(i):
        entry_copy(i).wait_send()
        state_copy(i).wait_send()
        state_arrival(i).wait_recv()

    @pl.loop(1, owners)
    def _(i):
        request_copy(i).wait_send()
        row_copy(i).wait_send()
        row_arrival(i).wait_recv()


def convolve_kernel(
    rows_ref,
    placed_ref,
    weight_ref,
    where_ref,
    carried_ref,
    filters_ref,
    gain_ref,
    out_ref,
    wide_rows,
    places,
    place_sem,
    weights_in,
    stage,
    even_in,
    odd_in,
):
    f32, bf16 = jnp.float32, jnp.bfloat16
    bag, slots = weight_ref.shape
    width = rows_ref.shape[1]
    channels = out_ref.shape[1]
    layers = filters_ref.shape[0]
    head = even_in.shape[0] - slots
    tile = 512
    moves = [
        pltpu.make_async_copy(
            placed_ref.at[k], places.at[pl.ds(k * slots, slots)], place_sem.at[k]
        )
        for k in range(bag)
    ]
    for move in moves:
        move.start()
    weights_in[...] = jnp.transpose(weight_ref[...])

    @pl.loop(0, rows_ref.shape[0] // tile)
    def _(i):
        at = pl.multiple_of(i * tile, tile)
        wide_rows[pl.ds(at, tile), :] = rows_ref[pl.ds(at, tile), :].astype(f32)

    for move in moves:
        move.wait()

    @pl.loop(0, slots // 8)
    def _(i):
        base = pl.multiple_of(i * 8, 8)
        for k in range(bag):
            for j in range(8):
                stage[k * 8 + j : k * 8 + j + 1, :] = wide_rows[
                    pl.ds(places[k * slots + base + j], 1), :
                ]
        weights = weights_in[pl.ds(base, 8), :]
        terms = [stage[k * 8 : k * 8 + 8, :] * weights[:, k : k + 1] for k in range(bag)]
        sums = (
            terms[0],
            terms[1],
            terms[2] + terms[3],
            (terms[4] + terms[5]) + (terms[6] + terms[7]),
        )
        for t in range(4):
            even_in[pl.ds(head + base, 8), t * width : (t + 1) * width] = (
                sums[t].astype(bf16).astype(f32)
            )

    state = carried_ref[where_ref[0]].astype(f32)
    state = jnp.where(where_ref[1] > 0, state, 0.0)
    block = 256
    offset = 0
    for layer in range(layers):
        dilation = 2**layer
        span = 2 * dilation
        source, target = (even_in, odd_in) if layer % 2 == 0 else (odd_in, even_in)
        source[head - span : head, :] = state[offset : offset + span, :]
        offset = offset + span
        for part in range(slots // block):
            low = head + part * block
            taps = [
                source[low - tap * dilation : low - tap * dilation + block, :].astype(bf16)
                for tap in range(3)
            ]
            values = jnp.dot(
                jnp.concatenate(taps, axis=1), filters_ref[layer], preferred_element_type=f32
            )
            mean = jnp.mean(values, axis=-1, keepdims=True)
            centred = values - mean
            spread = jnp.mean(centred * centred, axis=-1, keepdims=True)
            active = jnp.maximum(
                centred * lax.rsqrt(spread + epsilon) * gain_ref[layer : layer + 1, :], 0.0
            )
            if layer % 2 == 1:
                active = active + target[low : low + block, :]
            if layer == layers - 1:
                out_ref[part * block : (part + 1) * block, :] = active.astype(bf16)
            else:
                target[low : low + block, :] = active.astype(bf16).astype(f32)


def convolve_call(rows, placed, weights, where, carried, filters, gain):
    bf16, f32 = jnp.bfloat16, jnp.float32
    bag, slots = placed.shape
    width, channels = rows.shape[1], carried.shape[2]
    return pl.pallas_call(
        convolve_kernel,
        out_shape=jax.ShapeDtypeStruct((slots, channels), bf16),
        in_specs=[
            whole(),
            whole(),
            whole(),
            whole(pltpu.SMEM),
            whole(),
            whole(),
            whole(),
        ],
        out_specs=whole(),
        scratch_shapes=[
            pltpu.VMEM((rows.shape[0], width), f32),
            pltpu.SMEM((bag * slots,), jnp.int32),
            pltpu.SemaphoreType.DMA((bag,)),
            pltpu.VMEM((slots, bag), f32),
            pltpu.VMEM((8 * bag, width), f32),
            pltpu.VMEM((32 + slots, channels), f32),
            pltpu.VMEM((32 + slots, channels), f32),
        ],
        compiler_params=pltpu.CompilerParams(vmem_limit_bytes=48 * MIB),
        name="convolve",
    )(rows, placed, weights, where, carried, filters, gain)


def local(
    bag_rows, bag_owner, bag_weight, tables, returning, home, entry, stores, conv_weight, norm_gain
):
    i32, f32, bf16 = jnp.int32, jnp.float32, jnp.bfloat16
    owners = lax.axis_size("table")
    peers = lax.axis_size("rep")
    slots, bag = bag_rows.shape[1:]
    shard_rows, width = tables.shape[1:]
    layers, _, channels = conv_weight.shape
    capacity = min(slots, (3 * slots * bag + 2 * owners - 1) // (2 * owners))
    entries, state_len = stores.shape[:2]
    state_rows = 32

    half, quarter = conv_weight.shape[1], channels // 4
    side, spots = 8, peers // 2
    dma = pltpu.SemaphoreType.DMA
    placed, rows, carried, filters = pl.pallas_call(
        functools.partial(exchange_kernel, shard_rows, capacity),
        out_shape=(
            jax.ShapeDtypeStruct((bag, slots), i32),
            jax.ShapeDtypeStruct((owners, capacity, width), bf16),
            jax.ShapeDtypeStruct((peers, state_rows, channels), bf16),
            jax.ShapeDtypeStruct((layers, owners * half, channels), bf16),
        ),
        in_specs=[whole(), whole(), whole(), whole(pl.ANY), whole(pl.ANY), whole()],
        out_specs=(whole(), whole(pl.ANY), whole(pl.ANY), whole()),
        scratch_shapes=[
            pltpu.VMEM((4 * shard_rows, width), bf16),
            pltpu.VMEM((state_len, entries, channels), bf16),
            pltpu.VMEM((4 * shard_rows, width), f32),
            pltpu.VMEM((state_len, entries, channels), f32),
            pltpu.VMEM((state_rows, channels), f32),
            pltpu.VMEM((capacity, width), f32),
            pltpu.VMEM((owners, capacity, width), bf16),
            pltpu.VMEM((owners, 256), i32),
            pltpu.VMEM((owners, 256), i32),
            pltpu.SMEM((owners, 256), i32),
            pltpu.VMEM((peers, 128), i32),
            pltpu.SMEM((peers, 128), i32),
            pltpu.VMEM((peers, state_rows, channels), bf16),
            pltpu.VMEM((peers, 2 * half, quarter), bf16),
            pltpu.VMEM((peers, owners, 2 * half, quarter), bf16),
            dma((owners,)),
            dma((owners,)),
            dma((owners,)),
            dma((owners,)),
            dma((peers,)),
            dma((peers,)),
            dma((peers,)),
            dma((peers,)),
            dma((side,)),
            dma((side,)),
            dma((side,)),
            dma((side,)),
            dma((spots, side)),
            dma((spots, side)),
            dma((spots, side)),
            dma((spots, side)),
            dma((4,)),
        ],
        compiler_params=pltpu.CompilerParams(
            collective_id=0, has_side_effects=True, vmem_limit_bytes=48 * MIB
        ),
        name="exchange",
    )(
        bag_owner[0].T,
        bag_rows[0].T,
        jnp.broadcast_to(entry[:, None], (1, 128)),
        tables.reshape(4 * shard_rows, width),
        jnp.transpose(stores, (1, 0, 2)),
        conv_weight,
    )

    hidden = convolve_call(
        rows.reshape(owners * capacity, width),
        placed,
        bag_weight[0].T,
        jnp.concatenate([home, returning]),
        carried,
        filters,
        norm_gain,
    )
    return hidden[None]


def solution(mesh):
    in_specs = (
        P(("table", "rep"), None, None),
        P(("table", "rep"), None, None),
        P(("table", "rep"), None, None),
        P(None, "table", None),
        P(("table", "rep")),
        P(("table", "rep")),
        P(("table", "rep")),
        P(("table", "rep"), None, None),
        P(None, "table", None),
        P(),
    )
    out_specs = P(("table", "rep"), None, None)
    return jax.shard_map(local, mesh=mesh, in_specs=in_specs, out_specs=out_specs, check_vma=False)
```

time: 199 us -> 157 us (0.79)
  the two profiles are of different devices: /device:TPU:6 before, /device:TPU:289 now
where the time goes in v2:
time: 157 us; the launch traced here: 156 us
  Pallas kernels  148 us (94%)
  local copies, waits for them, and re-layouts  6.39 us (4%)
  between operations  1.97 us (1%)
    pallas_call x1, Pallas kernels, local(): pl.pallas_call(functools.partial(exchange_kernel, shard_rows, capacity),...  125 us
    pallas_call x1, Pallas kernels, convolve_call(): pl.pallas_call(convolve_kernel, out_shape=jax.ShapeDtypeStruct((slots, ch...  22.6 us
    unnamed x14, local copies, waits for them, and re-layouts  6.39 us

profile of v2, /device:TPU:289, one launch (start us, length us, event | category | flops | bytes accessed | tf_op | source)
XLA Modules:
  0.0 156.0 jit_solution(11281590510195165551)
XLA Ops:
  1.9 0.1 pad_add_fusion.where_ref
  2.0 0.0 copy-start
  2.0 1.6 %copy-done = bf16[4,2048,128]{2,1,0:T(8,128)(2,1)S(1)} copy-done((bf16[4,2048,128]{2,1,0:T(8,128)(2,1)S(1)}, bf16[4,2048,128]{2,1,0:T(8,128)(2,1)}, u32[]{:S(2)}) %copy-start) | copy-done | bytes 2097176
  3.6 0.0 copy-start.1
  3.6 0.9 copy-done.1
  4.6 0.0 copy-start.2
  4.6 0.9 copy-done.2
  5.4 0.0 copy-start.3
  5.5 0.8 copy-done.3
  6.2 0.0 copy-start.4
  6.2 0.8 copy-done.4
  7.0 125.1 %exchange.1 = (s32[8,1024]{1,0:T(8,128)S(1)}, bf16[64,192,128]{2,1,0:T(8,128)(2,1)S(1)}, bf16[8,32,512]{2,1,0:T(8,128)(2,1)S(1)}, bf16[4,1536,512]{2,1,0:T(8,128)(2,1)}) custom-call(s32[8,1024]{1,0:T(8,128)S(1)} %bitcast.18, s32[8,1024]{1,0:T(8,128)S(1)} %bitcast.19, s32[1,128]{1,0:T(1,128)S(1)} %broadcast_in_dim.12.entry_ref, ...), custom_call_target="tpu_custom_call" | custom-call | tf_op jit(solution)/shard_map/exchange/pallas_call | solution.py:574
  132.0 0.0 copy-start.5
  132.0 0.7 copy-done.5
  132.8 0.0 copy-start.6
  132.8 0.7 copy-done.6
  133.5 22.6 %convolve.1 = bf16[1024,512]{1,0:T(8,128)(2,1)} custom-call(bf16[12288,128]{1,0:T(8,128)(2,1)S(1)} %bitcast.15, s32[8,1024]{1,0:T(8,128)S(1)} %get-tuple-element.10.placed_ref, f32[8,1024]{1,0:T(8,128)S(1)} %bitcast.20, s32[2]{0:T(128)S(1)} %pad_add_fusion.where_ref, bf16[8,32,512]{2,1,0:T(8,128)(2,1)S(1)} %get-tuple-element.11.carried_ref, ...), custom_call_target="tpu_custom_call" | custom-call | tf_op jit(solution)/shard_map/convolve/pallas_call | solution.py:531
  (1 shorter events, 0.0 us)
Async XLA Ops:
  2.0 1.6 %copy-start = (bf16[4,2048,128]{2,1,0:T(8,128)(2,1)S(1)}, bf16[4,2048,128]{2,1,0:T(8,128)(2,1)}, u32[]{:S(2)}) copy-start(bf16[4,2048,128]{2,1,0:T(8,128)(2,1)} %param.13) | copy-start | bytes 6291460
  3.6 0.9 copy-start.1
  4.6 0.9 copy-start.2
  5.4 0.8 copy-start.3
  6.2 0.8 copy-start.4
  132.0 0.8 copy-start.5
  132.8 0.7 copy-start.6

commit v3 on v2

--- a/solution.py
+++ b/solution.py
@@ -47,7 +47,8 @@
         owner = owner_ref[k : k + 1, :]
         hit = owner == owner_row
         rank = jnp.sum(jnp.where(hit, ranks, 0.0), axis=0, keepdims=True).astype(jnp.int32)
-        placed_ref[k : k + 1, :] = owner * capacity + rank
+        place = owner * capacity + rank
+        placed_ref[k : k + 1, :] = jnp.clip(place, 0, owners * capacity - 1)
         value = rows_ref[k : k + 1, :] + table_of_id[k] * shard_rows
         high = jnp.where(hit, (value >> 6).astype(f32), 0.0)
         low = jnp.where(hit, (value & 63).astype(f32), 0.0)
@@ -65,12 +66,12 @@
     capacity,
     owner_ref,
     bag_rows_ref,
+    weight_ref,
     entry_ref,
     table_ref,
     stores_ref,
     shard_ref,
-    placed_out,
-    rows_out,
+    pooled_out,
     carried_out,
     filters_out,
     table_here,
@@ -80,6 +81,12 @@
     state_stage,
     stage,
     send_rows,
+    rows_in,
+    flat_rows,
+    weights_in,
+    placed_ref,
+    places,
+    place_sem,
     req_ref,
     req_in,
     req_words,
@@ -108,6 +115,8 @@
 ):
     owners = req_ref.shape[0]
     peers = entry_in.shape[0]
+    bag, slots = owner_ref.shape
+    width = table_ref.shape[1]
     side = 8
     me = lax.axis_index("table")
     rep = lax.axis_index("rep")
@@ -169,11 +178,14 @@
 
     def row_copy(index):
         to = partner(index)
-        return remote(send_rows.at[to], rows_out.at[me], row_send.at[to], row_recv.at[me], to, rep)
+        return remote(send_rows.at[to], rows_in.at[me], row_send.at[to], row_recv.at[me], to, rep)
+
+    def row_send_to(to):
+        return remote(send_rows.at[to], rows_in.at[me], row_send.at[to], row_recv.at[me], to, rep)
 
     def row_arrival(index):
         source = origin(index)
-        block = rows_out.at[source]
+        block = rows_in.at[source]
         return remote(block, block, row_send.at[source], row_recv.at[source], source, rep)
 
     core = lax.rem(rep, 2)
@@ -264,7 +276,7 @@
     stores_move = pltpu.make_async_copy(stores_ref, stores_here, local_sem.at[3])
     stores_move.start()
 
-    route(shard_rows, capacity, owner_ref, bag_rows_ref, req_ref, placed_out)
+    route(shard_rows, capacity, owner_ref, bag_rows_ref, req_ref, placed_ref)
 
     half = shard_ref.shape[1]
     quarter = pieces.shape[2]
@@ -277,21 +289,29 @@
 
     pl.semaphore_wait(barrier, owners - 1 + peers - 1)
 
-    @pl.loop(1, owners)
-    def _(i):
-        request_copy(i).start()
-
-    @pl.loop(1, side)
-    def _(i):
-        near_copy(i).start()
-
-    @pl.loop(1, peers)
-    def _(i):
-        entry_copy(i).start()
-
+    gathered[rep, major * side + minor] = pieces[rep]
     req_in[pl.ds(me, 1), :] = req_ref[pl.ds(me, 1), :]
     entry_in[pl.ds(rep, 1), :] = entry_ref[...]
-    gathered[rep, major * side + minor] = pieces[rep]
+
+    @pl.loop(1, side)
+    def _(i):
+        near_copy(i).start()
+
+    @pl.loop(1, owners)
+    def _(i):
+        request_copy(i).start()
+
+    @pl.loop(1, peers)
+    def _(i):
+        entry_copy(i).start()
+
+    @pl.loop(1, side)
+    def _(i):
+        near_arrival(i).wait_recv()
+
+    @pl.loop(1, side)
+    def _(i):
+        far_copy(i).start()
 
     tile = 256
     table_move.wait()
@@ -300,14 +320,6 @@
     def _(i):
         at = pl.multiple_of(i * tile, tile)
         wide_table[pl.ds(at, tile), :] = table_here[pl.ds(at, tile), :].astype(jnp.float32)
-
-    @pl.loop(1, side)
-    def _(i):
-        near_arrival(i).wait_recv()
-
-    @pl.loop(1, side)
-    def _(i):
-        far_copy(i).start()
 
     @pl.loop(1, owners)
     def _(i):
@@ -322,13 +334,7 @@
             stage[u : u + 1, :] = wide_table[pl.ds(req_words[to, u], 1), :]
         send_rows[to] = stage[...].astype(jnp.bfloat16)
 
-    @pl.loop(1, owners)
-    def _(i):
-        gather(partner(i))
-        row_copy(i).start()
-
-    @pl.loop(0, side)
-    def _(i):
+    def pass_along(i):
         a = lax.rem(major + side - i, side)
 
         @pl.when(i > 0)
@@ -339,43 +345,87 @@
             line_copy(ahead, a).start()
         core_copy(0, a).start()
 
-    gather(me)
-    own_rows = pltpu.make_async_copy(send_rows.at[me], rows_out.at[me], local_sem.at[0])
-    own_rows.start()
-
-    stores_move.wait()
-    wide_stores[...] = stores_here[...].astype(jnp.float32)
-    state_stage[...] = jnp.zeros_like(state_stage)
-
-    @pl.loop(1, peers)
-    def _(i):
-        entry_arrival(i).wait_recv()
-
-    entry_move = pltpu.make_async_copy(entry_in, entry_words, local_sem.at[1])
-    entry_move.start()
-    entry_move.wait()
-
-    @pl.loop(0, peers)
-    def _(i):
-        to = lax.rem(rep + i, peers)
-        chosen = entry_words[to, 0]
-        for row in range(stores_here.shape[0]):
-            state_stage[row : row + 1, :] = wide_stores[row, pl.ds(chosen, 1), :]
-        send_state[to] = state_stage[...].astype(jnp.bfloat16)
-
-    @pl.loop(1, peers)
-    def _(i):
-        state_copy(i).start()
-
-    own_state = pltpu.make_async_copy(send_state.at[rep], carried_out.at[rep], local_sem.at[1])
-    own_state.start()
-
-    @pl.loop(0, side)
-    def _(i):
+    def pass_over(i):
         a = lax.rem(major + side - i, side)
         for ahead in range(1, spots):
             line_arrival(ahead, a).wait_recv()
             core_copy(ahead, a).start()
+
+    def send_states():
+        stores_move.wait()
+        wide_stores[...] = stores_here[...].astype(jnp.float32)
+        state_stage[...] = jnp.zeros_like(state_stage)
+
+        @pl.loop(1, peers)
+        def _(i):
+            entry_arrival(i).wait_recv()
+
+        entry_move = pltpu.make_async_copy(entry_in, entry_words, local_sem.at[1])
+        entry_move.start()
+        entry_move.wait()
+
+        @pl.loop(0, peers)
+        def _(i):
+            to = lax.rem(rep + i, peers)
+            chosen = entry_words[to, 0]
+            for row in range(stores_here.shape[0]):
+                state_stage[row : row + 1, :] = wide_stores[row, pl.ds(chosen, 1), :]
+            send_state[to] = state_stage[...].astype(jnp.bfloat16)
+
+        @pl.loop(1, peers)
+        def _(i):
+            state_copy(i).start()
+
+    @pl.loop(0, owners)
+    def _(i):
+        group = i // 4
+        turn = lax.rem(i, 4)
+        long, short = group // 4 + 1, lax.rem(group, 4)
+        odd, back = lax.rem(turn, 2), turn // 2
+        ahead_z = (1 - 2 * back) * (long + odd * (short - long))
+        ahead_y = (1 - 2 * back) * (short - odd * (short + long))
+        straight = jnp.where((group == 12) & (turn == 2), 1, 0)
+        ahead_z = ahead_z + side + straight * (4 - ahead_z - side)
+        ahead_y = ahead_y + side + straight * (4 - ahead_y - side)
+
+        @pl.when((group != 12) | (turn < 3))
+        def _():
+            to = lax.rem(my_z + ahead_z, side) * side + lax.rem(my_y + ahead_y, side)
+            gather(to)
+            row_send_to(to).start()
+
+    @pl.loop(0, side)
+    def _(i):
+        pass_along(i)
+
+    gather(me)
+    own_rows = pltpu.make_async_copy(send_rows.at[me], rows_in.at[me], local_sem.at[0])
+    own_rows.start()
+    send_states()
+    own_state = pltpu.make_async_copy(send_state.at[rep], carried_out.at[rep], local_sem.at[1])
+    own_state.start()
+
+    moves = [
+        pltpu.make_async_copy(
+            placed_ref.at[k], places.at[pl.ds(k * slots, slots)], place_sem.at[k]
+        )
+        for k in range(bag)
+    ]
+    for move in moves:
+        move.start()
+    weights_in[...] = jnp.transpose(weight_ref[...])
+    for move in moves:
+        move.wait()
+    def widen(source):
+        at = pl.multiple_of(source * capacity, capacity)
+        flat_rows[pl.ds(at, capacity), :] = rows_in[source].astype(jnp.float32)
+
+    own_rows.wait()
+    widen(me)
+
+    @pl.loop(0, side)
+    def _(i):
+        pass_over(i)
 
     @pl.loop(0, side)
     def _(a):
@@ -400,84 +450,17 @@
                 [first[half:], second[half:]], axis=0
             )
 
-    @pl.loop(1, side)
-    def _(i):
-        near_copy(i).wait_send()
-        far_copy(i).wait_send()
-
-    @pl.loop(0, side)
-    def _(a):
-        for ahead in range(1, spots):
-            line_copy(ahead, a).wait_send()
-        for ahead in range(spots):
-            core_copy(ahead, a).wait_send()
-
-    own_rows.wait()
-    own_state.wait()
-
-    @pl.loop(1, peers)
-    def _(i):
-        entry_copy(i).wait_send()
-        state_copy(i).wait_send()
-        state_arrival(i).wait_recv()
-
     @pl.loop(1, owners)
     def _(i):
-        request_copy(i).wait_send()
-        row_copy(i).wait_send()
         row_arrival(i).wait_recv()
-
-
-def convolve_kernel(
-    rows_ref,
-    placed_ref,
-    weight_ref,
-    where_ref,
-    carried_ref,
-    filters_ref,
-    gain_ref,
-    out_ref,
-    wide_rows,
-    places,
-    place_sem,
-    weights_in,
-    stage,
-    even_in,
-    odd_in,
-):
-    f32, bf16 = jnp.float32, jnp.bfloat16
-    bag, slots = weight_ref.shape
-    width = rows_ref.shape[1]
-    channels = out_ref.shape[1]
-    layers = filters_ref.shape[0]
-    head = even_in.shape[0] - slots
-    tile = 512
-    moves = [
-        pltpu.make_async_copy(
-            placed_ref.at[k], places.at[pl.ds(k * slots, slots)], place_sem.at[k]
-        )
-        for k in range(bag)
-    ]
-    for move in moves:
-        move.start()
-    weights_in[...] = jnp.transpose(weight_ref[...])
-
-    @pl.loop(0, rows_ref.shape[0] // tile)
-    def _(i):
-        at = pl.multiple_of(i * tile, tile)
-        wide_rows[pl.ds(at, tile), :] = rows_ref[pl.ds(at, tile), :].astype(f32)
-
-    for move in moves:
-        move.wait()
-
-    @pl.loop(0, slots // 8)
-    def _(i):
+        widen(origin(i))
+
+    def pool(i):
         base = pl.multiple_of(i * 8, 8)
         for k in range(bag):
             for j in range(8):
-                stage[k * 8 + j : k * 8 + j + 1, :] = wide_rows[
-                    pl.ds(places[k * slots + base + j], 1), :
-                ]
+                place = places[base + (k * slots + j)]
+                stage[k * 8 + j : k * 8 + j + 1, :] = flat_rows[pl.ds(place, 1), :]
         weights = weights_in[pl.ds(base, 8), :]
         terms = [stage[k * 8 : k * 8 + 8, :] * weights[:, k : k + 1] for k in range(bag)]
         sums = (
@@ -487,10 +470,48 @@
             (terms[4] + terms[5]) + (terms[6] + terms[7]),
         )
         for t in range(4):
-            even_in[pl.ds(head + base, 8), t * width : (t + 1) * width] = (
-                sums[t].astype(bf16).astype(f32)
+            pooled_out[pl.ds(base, 8), t * width : (t + 1) * width] = (
+                sums[t].astype(jnp.bfloat16).astype(jnp.float32)
             )
 
+    @pl.loop(0, slots // 8)
+    def _(i):
+        pool(i)
+
+    @pl.loop(1, side)
+    def _(i):
+        near_copy(i).wait_send()
+        far_copy(i).wait_send()
+
+    @pl.loop(0, side)
+    def _(a):
+        for ahead in range(1, spots):
+            line_copy(ahead, a).wait_send()
+        for ahead in range(spots):
+            core_copy(ahead, a).wait_send()
+
+    own_state.wait()
+
+    @pl.loop(1, peers)
+    def _(i):
+        entry_copy(i).wait_send()
+        state_copy(i).wait_send()
+        state_arrival(i).wait_recv()
+
+    @pl.loop(1, owners)
+    def _(i):
+        request_copy(i).wait_send()
+        row_copy(i).wait_send()
+
+
+def convolve_kernel(
+    pooled_ref, where_ref, carried_ref, filters_ref, gain_ref, out_ref, even_in, odd_in
+):
+    f32, bf16 = jnp.float32, jnp.bfloat16
+    slots = pooled_ref.shape[0]
+    layers = filters_ref.shape[0]
+    head = even_in.shape[0] - slots
+    even_in[head:, :] = pooled_ref[...]
     state = carried_ref[where_ref[0]].astype(f32)
     state = jnp.where(where_ref[1] > 0, state, 0.0)
     block = 256
@@ -524,37 +545,6 @@
                 target[low : low + block, :] = active.astype(bf16).astype(f32)
 
 
-def convolve_call(rows, placed, weights, where, carried, filters, gain):
-    bf16, f32 = jnp.bfloat16, jnp.float32
-    bag, slots = placed.shape
-    width, channels = rows.shape[1], carried.shape[2]
-    return pl.pallas_call(
-        convolve_kernel,
-        out_shape=jax.ShapeDtypeStruct((slots, channels), bf16),
-        in_specs=[
-            whole(),
-            whole(),
-            whole(),
-            whole(pltpu.SMEM),
-            whole(),
-            whole(),
-            whole(),
-        ],
-        out_specs=whole(),
-        scratch_shapes=[
-            pltpu.VMEM((rows.shape[0], width), f32),
-            pltpu.SMEM((bag * slots,), jnp.int32),
-            pltpu.SemaphoreType.DMA((bag,)),
-            pltpu.VMEM((slots, bag), f32),
-            pltpu.VMEM((8 * bag, width), f32),
-            pltpu.VMEM((32 + slots, channels), f32),
-            pltpu.VMEM((32 + slots, channels), f32),
-        ],
-        compiler_params=pltpu.CompilerParams(vmem_limit_bytes=48 * MIB),
-        name="convolve",
-    )(rows, placed, weights, where, carried, filters, gain)
-
-
 def local(
     bag_rows, bag_owner, bag_weight, tables, returning, home, entry, stores, conv_weight, norm_gain
 ):
@@ -571,16 +561,15 @@
     half, quarter = conv_weight.shape[1], channels // 4
     side, spots = 8, peers // 2
     dma = pltpu.SemaphoreType.DMA
-    placed, rows, carried, filters = pl.pallas_call(
+    pooled, carried, filters = pl.pallas_call(
         functools.partial(exchange_kernel, shard_rows, capacity),
         out_shape=(
-            jax.ShapeDtypeStruct((bag, slots), i32),
-            jax.ShapeDtypeStruct((owners, capacity, width), bf16),
+            jax.ShapeDtypeStruct((slots, 4 * width), f32),
             jax.ShapeDtypeStruct((peers, state_rows, channels), bf16),
             jax.ShapeDtypeStruct((layers, owners * half, channels), bf16),
         ),
-        in_specs=[whole(), whole(), whole(), whole(pl.ANY), whole(pl.ANY), whole()],
-        out_specs=(whole(), whole(pl.ANY), whole(pl.ANY), whole()),
+        in_specs=[whole(), whole(), whole(), whole(), whole(pl.ANY), whole(pl.ANY), whole()],
+        out_specs=(whole(), whole(pl.ANY), whole()),
         scratch_shapes=[
             pltpu.VMEM((4 * shard_rows, width), bf16),
             pltpu.VMEM((state_len, entries, channels), bf16),
@@ -589,6 +578,12 @@
             pltpu.VMEM((state_rows, channels), f32),
             pltpu.VMEM((capacity, width), f32),
             pltpu.VMEM((owners, capacity, width), bf16),
+            pltpu.VMEM((owners, capacity, width), bf16),
+            pltpu.VMEM((owners * capacity, width), f32),
+            pltpu.VMEM((slots, bag), f32),
+            pltpu.VMEM((bag, slots), i32),
+            pltpu.SMEM((bag * slots,), i32),
+            dma((bag,)),
             pltpu.VMEM((owners, 256), i32),
             pltpu.VMEM((owners, 256), i32),
             pltpu.SMEM((owners, 256), i32),
@@ -622,21 +617,25 @@
     )(
         bag_owner[0].T,
         bag_rows[0].T,
+        bag_weight[0].T,
         jnp.broadcast_to(entry[:, None], (1, 128)),
         tables.reshape(4 * shard_rows, width),
         jnp.transpose(stores, (1, 0, 2)),
         conv_weight,
     )
 
-    hidden = convolve_call(
-        rows.reshape(owners * capacity, width),
-        placed,
-        bag_weight[0].T,
-        jnp.concatenate([home, returning]),
-        carried,
-        filters,
-        norm_gain,
-    )
+    hidden = pl.pallas_call(
+        convolve_kernel,
+        out_shape=jax.ShapeDtypeStruct((slots, channels), bf16),
+        in_specs=[whole(), whole(pltpu.SMEM), whole(), whole(), whole()],
+        out_specs=whole(),
+        scratch_shapes=[
+            pltpu.VMEM((32 + slots, channels), f32),
+            pltpu.VMEM((32 + slots, channels), f32),
+        ],
+        compiler_params=pltpu.CompilerParams(vmem_limit_bytes=40 * MIB),
+        name="convolve",
+    )(pooled, jnp.concatenate([home, returning]), carried, filters, norm_gain)
     return hidden[None]
 
 

time: 157 us -> 152 us (0.968)
  the two profiles are of different devices: /device:TPU:289 before, /device:TPU:313 now
where the time goes in v3:
time: 152 us
  Pallas kernels  141 us (93%)
  local copies, waits for them, and re-layouts  8.48 us (6%)
  between operations  1.99 us (1%)
    pallas_call x1, Pallas kernels, local(): pl.pallas_call(functools.partial(exchange_kernel, shard_rows, capacity),...  132 us
    pallas_call x1, Pallas kernels, local(): pl.pallas_call(convolve_kernel, out_shape=jax.ShapeDtypeStruct((slots, ch...  8.62 us
    unnamed x16, local copies, waits for them, and re-layouts  8.48 us

profile of v3, /device:TPU:313, one launch (start us, length us, event | category | flops | bytes accessed | tf_op | source)
XLA Modules:
  0.0 151.5 jit_solution(11211634712264322688)
XLA Ops:
  0.0 0.0 copy-start.7
  2.0 0.1 pad_add_fusion.where_ref
  2.0 0.0 copy-start.1
  2.0 1.6 %copy-done.1 = bf16[4,2048,128]{2,1,0:T(8,128)(2,1)S(1)} copy-done((bf16[4,2048,128]{2,1,0:T(8,128)(2,1)S(1)}, bf16[4,2048,128]{2,1,0:T(8,128)(2,1)}, u32[]{:S(2)}) %copy-start.1) | copy-done | bytes 2097176
  3.6 0.0 copy-start.2
  3.6 0.9 copy-done.2
  4.6 0.0 copy-start.3
  4.6 0.9 copy-done.3
  5.5 0.0 copy-start.4
  5.5 0.8 copy-done.4
  6.2 0.0 copy-start.5
  6.2 0.8 copy-done.5
  7.0 0.0 copy-start.6
  7.0 0.8 copy-done.6
  7.7 132.4 %exchange.1 = (f32[1024,512]{1,0:T(8,128)S(1)}, bf16[8,32,512]{2,1,0:T(8,128)(2,1)S(1)}, bf16[4,1536,512]{2,1,0:T(8,128)(2,1)}) custom-call(s32[8,1024]{1,0:T(8,128)S(1)} %bitcast.16, s32[8,1024]{1,0:T(8,128)S(1)} %bitcast.17, f32[8,1024]{1,0:T(8,128)S(1)} %bitcast.18, s32[1,128]{1,0:T(1,128)S(1)} %broadcast_in_dim.12.entry_ref, ...), custom_call_target="tpu_custom_call" | custom-call | tf_op jit(solution)/shard_map/exchange/pallas_call | solution.py:564
  140.1 0.0 copy-done.7
  140.1 0.0 copy-start
  140.1 2.8 %copy-done = bf16[4,1536,512]{2,1,0:T(8,128)(2,1)S(1)} copy-done((bf16[4,1536,512]{2,1,0:T(8,128)(2,1)S(1)}, bf16[4,1536,512]{2,1,0:T(8,128)(2,1)}, u32[]{:S(2)}) %copy-start) | copy-done | bytes 6291480
  142.9 8.6 %convolve.1 = bf16[1024,512]{1,0:T(8,128)(2,1)} custom-call(f32[1024,512]{1,0:T(8,128)S(1)} %get-tuple-element.8.pooled_ref, s32[2]{0:T(128)S(1)} %pad_add_fusion.where_ref, bf16[8,32,512]{2,1,0:T(8,128)(2,1)S(1)} %get-tuple-element.9.carried_ref, bf16[4,1536,512]{2,1,0:T(8,128)(2,1)S(1)} %copy-done, f32[4,512]{1,0:T(4,128)S(1)} %copy-done.7), custom_call_target="tpu_custom_call" | custom-call | tf_op jit(solution)/shard_map/convolve/pallas_call | solution.py:627
  (1 shorter events, 0.0 us)
Async XLA Ops:
  0.0 140.1 %copy-start.7 = (f32[4,512]{1,0:T(4,128)S(1)}, f32[4,512]{1,0:T(4,128)}, u32[]{:S(2)}) copy-start(f32[4,512]{1,0:T(4,128)} %gain_ref.1) | copy-start | bytes 24580
  2.0 1.6 %copy-start.1 = (bf16[4,2048,128]{2,1,0:T(8,128)(2,1)S(1)}, bf16[4,2048,128]{2,1,0:T(8,128)(2,1)}, u32[]{:S(2)}) copy-start(bf16[4,2048,128]{2,1,0:T(8,128)(2,1)} %param.13) | copy-start | bytes 6291460
  3.6 0.9 copy-start.2
  4.6 0.9 copy-start.3
  5.5 0.8 copy-start.4
  6.2 0.8 copy-start.5
  7.0 0.8 copy-start.6
  140.1 2.8 %copy-start = (bf16[4,1536,512]{2,1,0:T(8,128)(2,1)S(1)}, bf16[4,1536,512]{2,1,0:T(8,128)(2,1)}, u32[]{:S(2)}) copy-start(bf16[4,1536,512]{2,1,0:T(8,128)(2,1)} %get-tuple-element.10.filters_ref) | copy-start | bytes 18874372
